TPU v7x, 128 devices: a whole 4x4x4 slice. The times are simulated.
128 devices in a mesh: rep: 8 (over x, z_lo), tp: 16 (over z_hi, y, core).
Axes of the slice: x: 4, y: 4, z: 4 (z_hi: 2, z_lo: 2; z = z_hi * 2 + z_lo), core: 2. Of those that a mesh axis runs over, the one named last changes fastest.
Arguments:
- pool_tokens: bfloat16 [1024, 4096], P('tp'), may hold values from -6 to 6
- pool_targets: bfloat16 [1024, 4096], P('tp'), may hold values from -6 to 6
- pick: int32 [8, 2, 384], P('rep', None, 'tp'), may hold values from 0 to 63
- up_weight: bfloat16 [4096, 14336], P(None, 'tp'), may hold values from -6 to 6
- down_weight: bfloat16 [14336, 4096], P('tp'), may hold values from -6 to 6
Outputs:
- new_down: bfloat16 [14336, 4096], P('tp')
Inputs may be any that keep to these rules, and one draw needn't show every extreme that they name: pick[r, s, t] counts from the first of the 64 pool rows held on the same tp index as token t.
All inputs are finite; a program needn't handle non-finite values.
Results may differ from a plain program's by a relative error of at most 0.011.
Values may be sent and summed in bfloat16 or wider, within the bound.
A program may use at most 128 MiB of HBM per device.

v0:
```python
import math

import jax
import jax.numpy as jnp
from jax import lax
from jax.sharding import PartitionSpec as P


def silu_slope(preact):
    sigma = jax.nn.sigmoid(preact)
    return sigma * (1.0 + preact * (1.0 - sigma))


def adamw(weight, grad, first, second, count):
    first = 0.9 * first + 0.1 * grad
    second = 0.95 * second + 0.05 * grad * grad
    first_hat = first / (1.0 - 0.9**count)
    second_hat = second / (1.0 - 0.95**count)
    weight = weight - 0.25 * (first_hat / (jnp.sqrt(second_hat) + 0.02) + 0.1 * weight)
    return (weight, first, second)


def outer_step(start_weight, average):
    return start_weight - 0.7 * (average + 0.9 * average)


def per_device(pool_tokens, pool_targets, pick, up_weight, down_weight):
    width = up_weight.shape[0]
    hid_dev = up_weight.shape[1]
    replicas = lax.axis_size("rep")
    scale_up = 1.0 / math.sqrt(width)
    scale_down = 1.0 / math.sqrt(hid_dev * lax.axis_size("tp"))
    chosen = pick[0]
    local_tokens = [jnp.take(pool_tokens, chosen[which], axis=0) for which in range(2)]
    local_goals = [jnp.take(pool_targets, chosen[which], axis=0) for which in range(2)]

    def gather_tokens(local):
        return lax.all_gather(local, "tp", axis=0, tiled=True)

    def forward(which, up_cast, down_cast):
        inputs = gather_tokens(local_tokens[which])
        preact = scale_up * jnp.dot(inputs, up_cast, preferred_element_type=jnp.float32)
        hidden = jax.nn.silu(preact).astype(jnp.bfloat16)
        mine = lax.psum_scatter(
            (scale_down * jnp.dot(hidden, down_cast, preferred_element_type=jnp.float32)).astype(
                jnp.bfloat16
            ),
            "tp",
            scatter_dimension=0,
            tiled=True,
        ).astype(jnp.float32)
        output = local_tokens[which].astype(jnp.float32) + mine
        error = (output - local_goals[which].astype(jnp.float32)).astype(jnp.bfloat16)
        error_all = lax.all_gather(error, "tp", axis=0, tiled=True)
        grad_down = scale_down * lax.dot_general(
            hidden, error_all, (((0,), (0,)), ((), ())), preferred_element_type=jnp.float32
        )
        return (inputs, preact, error_all, grad_down)

    inputs, preact, error_all, grad_down = forward(0, up_weight, down_weight)
    slope_pre = scale_down * lax.dot_general(
        error_all, down_weight, (((1,), (1,)), ((), ())), preferred_element_type=jnp.float32
    )
    slope = (slope_pre * silu_slope(preact)).astype(jnp.bfloat16)
    grad_up = scale_up * lax.dot_general(
        inputs, slope, (((0,), (0,)), ((), ())), preferred_element_type=jnp.float32
    )
    up_master = up_weight.astype(jnp.float32)
    down_start = down_weight.astype(jnp.float32)
    zeros_up = jnp.zeros(up_master.shape, jnp.float32)
    zeros_down = jnp.zeros(down_start.shape, jnp.float32)
    up_master, first_up, second_up = adamw(up_master, grad_up, zeros_up, zeros_up, 1)
    down_master, first_down, second_down = adamw(down_start, grad_down, zeros_down, zeros_down, 1)
    inputs, preact, error_all, grad_down = forward(
        1, up_master.astype(jnp.bfloat16), down_master.astype(jnp.bfloat16)
    )
    down_master, first_down, second_down = adamw(down_master, grad_down, first_down, second_down, 2)
    delta = down_start - down_master
    average = lax.psum(delta.astype(jnp.bfloat16), "rep").astype(jnp.float32) / replicas
    return outer_step(down_start, average).astype(jnp.bfloat16)


def solution(mesh):
    in_specs = (P("tp", None), P("tp", None), P("rep", None, "tp"), P(None, "tp"), P("tp", None))
    out_specs = P("tp", None)
    return jax.shard_map(
        per_device, mesh=mesh, in_specs=in_specs, out_specs=out_specs, check_vma=False
    )
```

profile of v0, /device:TPU:0, one launch (start us, length us, event | category | flops | bytes accessed | tf_op | source)
XLA Modules:
  0.0 775.3 jit_solution(10116646741631646538)
XLA Ops:
  6.5 0.8 compare_and_fusion.1
  7.6 0.7 gather_fusion
  8.3 0.8 broadcast_select_fusion.1
  9.1 55.6 %all-gather.5.cloned.1.call-done = bf16[384,4096]{1,0:T(8,128)(2,1)} async-done(((bf16[24,4096]{1,0:T(8,128)(2,1)}), bf16[384,4096]{1,0:T(8,128)(2,1)}) %all-gather.5.cloned.1.call-update) | async-done | bytes 3145744 | tf_op jit(solution)/shard_map/all_gather | solution.py:38
  64.7 8.0 %convolution_multiply_fusion.1 = f32[384,896]{1,0:T(8,128)S(1)} fusion(bf16[384,4096]{1,0:T(8,128)(2,1)} %all-gather.5.cloned.1.call-done, bf16[4096,896]{1,0:T(8,128)(2,1)} %param.10), kind=kOutput, calls=%fused_computation.27 | convolution fusion | flops 2818916352 | bytes 11862016 | tf_op jit(solution)/shard_map/dot_general | solution.py:42
  72.7 8.0 %multiply_convert_fusion.1 = bf16[384,4096]{1,0:T(8,128)(2,1)} fusion(bf16[896,4096]{1,0:T(8,128)(2,1)} %param.11, f32[384,896]{1,0:T(8,128)S(1)} %convolution_multiply_fusion.1), kind=kOutput, calls=%fused_computation.23 | convolution fusion | flops 2823438336 | bytes 11862016 | tf_op jit(solution)/shard_map/dot_general | solution.py:45
  80.7 0.7 gather_fusion.1
  81.4 73.4 %reduce-scatter.3.cloned.1.call-done = bf16[24,4096]{1,0:T(8,128)(2,1)} async-done(((bf16[384,4096]{1,0:T(8,128)(2,1)}), bf16[24,4096]{1,0:T(8,128)(2,1)}) %reduce-scatter.3.cloned.1.call-update) | async-done | bytes 196624 | tf_op jit(solution)/shard_map/reduce_scatter | solution.py:44
  154.8 1.8 subtract_convert_fusion.1
  156.6 0.7 gather_fusion.2
  157.3 0.8 broadcast_select_fusion
  158.3 50.0 %all-gather.7.cloned.1.call-done = bf16[384,4096]{1,0:T(8,128)(2,1)} async-done(((bf16[24,4096]{1,0:T(8,128)(2,1)}), bf16[384,4096]{1,0:T(8,128)(2,1)}) %all-gather.7.cloned.1.call-update) | async-done | bytes 3145744 | tf_op jit(solution)/shard_map/all_gather | solution.py:54
  208.3 11.3 %fusion.34 = f32[896,4096]{1,0:T(8,128)} fusion(bf16[384,4096]{1,0:T(8,128)(2,1)} %all-gather.7.cloned.1.call-done, f32[384,896]{1,0:T(8,128)S(1)} %convolution_multiply_fusion.1), kind=kOutput, calls=%fused_computation.55 | convolution fusion | flops 2820292608 | bytes 19202048 | tf_op jit(solution)/shard_map/dot_general | solution.py:55
  219.6 6.7 fusion.19
  226.3 35.3 %all-gather.9.cloned.1.call-done = bf16[384,4096]{1,0:T(8,128)(2,1)} async-done(((bf16[24,4096]{1,0:T(8,128)(2,1)}), bf16[384,4096]{1,0:T(8,128)(2,1)}) %all-gather.9.cloned.1.call-update) | async-done | bytes 3145744 | tf_op jit(solution)/shard_map/all_gather | solution.py:38
  261.6 21.7 %multiply_convert_fusion.2 = bf16[384,896]{1,0:T(8,128)(2,1)S(1)} fusion(bf16[384,4096]{1,0:T(8,128)(2,1)} %all-gather.9.cloned.1.call-done, bf16[4096,896]{1,0:T(8,128)(2,1)} %param.10, bf16[384,4096]{1,0:T(8,128)(2,1)} %all-gather.5.cloned.1.call-done, bf16[384,896]{1,0:T(8,128)(2,1)S(1)} %fusion.19), kind=kOutput, calls=%fused_computation.29 | convolution fusion | flops 5683249152 | bytes 15007744 | tf_op jit(solution)/shard_map/dot_general | solution.py:42
  283.3 16.8 %multiply_convert_fusion = bf16[384,4096]{1,0:T(8,128)(2,1)} fusion(bf16[384,896]{1,0:T(8,128)(2,1)S(1)} %multiply_convert_fusion.2, bf16[896,4096]{1,0:T(8,128)(2,1)} %param.11, f32[896,4096]{1,0:T(8,128)} %fusion.34), kind=kOutput, calls=%fused_computation.22 | convolution fusion | flops 2865758208 | bytes 25853952 | tf_op jit(solution)/shard_map/dot_general | solution.py:45
  300.2 0.7 gather_fusion.3
  300.9 73.3 %reduce-scatter.5.cloned.1.call-done = bf16[24,4096]{1,0:T(8,128)(2,1)} async-done(((bf16[384,4096]{1,0:T(8,128)(2,1)}), bf16[24,4096]{1,0:T(8,128)(2,1)}) %reduce-scatter.5.cloned.1.call-update) | async-done | bytes 196624 | tf_op jit(solution)/shard_map/reduce_scatter | solution.py:44
  374.2 1.8 subtract_convert_fusion
  376.1 51.5 %all-gather.11.cloned.1.call-done = bf16[384,4096]{1,0:T(8,128)(2,1)} async-done(((bf16[24,4096]{1,0:T(8,128)(2,1)}), bf16[384,4096]{1,0:T(8,128)(2,1)}) %all-gather.11.cloned.1.call-update) | async-done | bytes 3145744 | tf_op jit(solution)/shard_map/all_gather | solution.py:54
  427.6 29.2 %fusion.5 = bf16[896,4096]{1,0:T(8,128)(2,1)} fusion(bf16[896,4096]{1,0:T(8,128)(2,1)} %param.11, f32[896,4096]{1,0:T(8,128)} %fusion.34, bf16[384,896]{1,0:T(8,128)(2,1)S(1)} %multiply_convert_fusion.2, bf16[384,4096]{1,0:T(8,128)(2,1)} %all-gather.11.cloned.1.call-done), kind=kOutput, calls=%fused_computation.15 | convolution fusion | flops 2925002752 | bytes 33193984 | tf_op jit(solution)/shard_map/dot_general | solution.py:55
  456.8 299.0 %all-reduce.2.cloned.1.call-done = bf16[896,4096]{1,0:T(8,128)(2,1)} async-done(((bf16[896,4096]{1,0:T(8,128)(2,1)}), bf16[896,4096]{1,0:T(8,128)(2,1)}) %all-reduce.2.cloned.1.call-update) | async-done | bytes 7340048 | tf_op jit(solution)/shard_map/psum | solution.py:79
  755.8 12.4 %fusion.6 = bf16[896,4096]{1,0:T(8,128)(2,1)} fusion(bf16[896,4096]{1,0:T(8,128)(2,1)} %param.11, bf16[896,4096]{1,0:T(8,128)(2,1)} %all-reduce.2.cloned.1.call-done), kind=kLoop, calls=%fused_computation.16 | loop fusion | flops 22020096 | bytes 22020096 | tf_op jit(solution)/shard_map/convert_element_type | solution.py:80
  (24 shorter events, 0.9 us)
Async XLA Ops:
  6.5 1.1 copy-start
  6.5 58.1 %all-gather.5.cloned.1.call-start = ((), (), s32[]{:S(2)}) async-start(), calls=%async_computation.2 | async-start | bytes 3342336 | tf_op jit(solution)/shard_map/all_gather | solution.py:38
  9.1 145.7 %reduce-scatter.3.cloned.1.call-start = ((), (), s32[]{:S(2)}) async-start(), calls=%async_computation.3 | async-start | bytes 3342336 | tf_op jit(solution)/shard_map/reduce_scatter | solution.py:44
  72.7 8.1 %copy-start.2 = (bf16[64,4096]{1,0:T(8,128)(2,1)S(1)}, bf16[64,4096]{1,0:T(8,128)(2,1)}, u32[]{:S(2)}) copy-start(bf16[64,4096]{1,0:T(8,128)(2,1)} %param.8) | copy-start | bytes 1572868
  80.7 127.6 %all-gather.7.cloned.1.call-start = ((), (), s32[]{:S(2)}) async-start(), calls=%async_computation.4 | async-start | bytes 3342336 | tf_op jit(solution)/shard_map/all_gather | solution.py:54
  156.6 105.0 %all-gather.9.cloned.1.call-start = ((), (), s32[]{:S(2)}) async-start(), calls=%async_computation.5 | async-start | bytes 3342336 | tf_op jit(solution)/shard_map/all_gather | solution.py:38
  158.1 216.1 %reduce-scatter.5.cloned.1.call-start = ((), (), s32[]{:S(2)}) async-start(), calls=%async_computation.6 | async-start | bytes 3342336 | tf_op jit(solution)/shard_map/reduce_scatter | solution.py:44
  208.3 11.3 %copy-start.3 = (bf16[384,4096]{1,0:T(8,128)(2,1)S(1)}, bf16[384,4096]{1,0:T(8,128)(2,1)}, u32[]{:S(2)}) copy-start(bf16[384,4096]{1,0:T(8,128)(2,1)} %all-gather.7.cloned.1.call-done) | copy-start | bytes 9437188
  300.1 127.4 %all-gather.11.cloned.1.call-start = ((), (), s32[]{:S(2)}) async-start(), calls=%async_computation.7 | async-start | bytes 3342336 | tf_op jit(solution)/shard_map/all_gather | solution.py:54
  376.0 379.8 %all-reduce.2.cloned.1.call-start = ((), (), s32[]{:S(2)}) async-start(), calls=%async_computation.8 | async-start | bytes 14680064 | tf_op jit(solution)/shard_map/psum | solution.py:79
  456.8 311.4 %copy-start.1 = (bf16[64,4096]{1,0:T(8,128)(2,1)S(1)}, bf16[64,4096]{1,0:T(8,128)(2,1)}, u32[]{:S(2)}) copy-start(bf16[64,4096]{1,0:T(8,128)(2,1)} %param.7) | copy-start | bytes 1572868
Sparse Core Ops, SparseCore 0:
  9.8 54.8 all-gather.4
  80.8 73.9 reduce-scatter.2
  157.2 51.0 all-gather.6
  210.6 50.9 all-gather.8
  300.3 73.9 reduce-scatter.4
  376.5 51.0 all-gather.10
  456.9 298.8 all-reduce.1
where the time goes:
time: 784 us; the launch traced here: 775 us
  waiting for transfers between devices  638 us (81%)
  matrix products  102 us (13%)
  other arithmetic  18.2 us (2%)
  between operations  13.8 us (2%)
    psum x1, waiting for transfers between devices, per_device(): lax.psum(delta.astype(jnp.bfloat16), 'rep').astype(jnp.float32) / replicas  299 us
    reduce_scatter x2, waiting for transfers between devices, forward(): lax.psum_scatter((scale_down * jnp.dot(hidden, down_cast, preferred_eleme...  147 us
    all_gather x2, waiting for transfers between devices, forward(): error_all = lax.all_gather(error, 'tp', axis=0, tiled=True)  102 us
    all_gather x2, waiting for transfers between devices, gather_tokens(): return lax.all_gather(local, 'tp', axis=0, tiled=True)  90.9 us
    dot_general x2, matrix products, forward(): lax.dot_general(hidden, error_all, (((0,), (0,)), ((), ())), preferred_el...  40.5 us
    dot_general x2, matrix products, forward(): jnp.dot(inputs, up_cast, preferred_element_type=jnp.float32)  29.7 us
    dot_general x2, matrix products, forward(): jnp.dot(hidden, down_cast, preferred_element_type=jnp.float32)  24.8 us
  transfers between devices with their start and end apart: 7, of which 7 were waited for; matrix products, arithmetic and copies ran while one was open for 3% of the time, Pallas kernels for 0%

commit v1 on v0

v1 whole, which is shorter than its diff:
```python
import functools
import math

import jax
import jax.numpy as jnp
from jax import lax
from jax.experimental import pallas as pl
from jax.experimental.pallas import tpu as pltpu
from jax.sharding import PartitionSpec as P

MESH = pl.DeviceIdType.MESH
BF, F32 = jnp.bfloat16, jnp.float32

CORE = (0, 0, 0, 0, 1)
YP, YM = (0, 0, 0, 1, 0), (0, 0, 0, -1, 0)
ZH = (0, 0, 1, 0, 0)
XP, XM, X2, ZL = (1, 0, 0, 0, 0), (-1, 0, 0, 0, 0), (2, 0, 0, 0, 0), (0, 1, 0, 0, 0)
REP = (None, XP, XM, X2, ZL, (1, 1, 0, 0, 0), (-1, 1, 0, 0, 0), (2, 1, 0, 0, 0))

TOK = 48
HALF = 2048
ROWS = 384
SLICE = 256
CHUNKS = 4


def place():
    r, t = lax.axis_index("rep"), lax.axis_index("tp")
    return r // 2, r % 2, t // 8, (t // 2) % 4, t % 2


def rep_index(off):
    x, zl, _, _, _ = place()
    return ((x + off[0] + 4) % 4) * 2 + (zl + off[1]) % 2


def target(off):
    _, _, zh, y, core = place()
    tp = (((zh + off[2]) % 2) * 4 + (y + off[3] + 4) % 4) * 2 + (core + off[4]) % 2
    return (rep_index(off), tp)


class Sends:
    def __init__(self, send_sems, recv_sems):
        self.send_sems, self.recv_sems, self.count = send_sems, recv_sems, 0

    def __call__(self, src, dst, off):
        k = self.count
        self.count += 1
        copy = pltpu.make_async_remote_copy(
            src_ref=src,
            dst_ref=dst,
            send_sem=self.send_sems.at[k],
            recv_sem=self.recv_sems.at[k],
            device_id=target(off),
            device_id_type=MESH,
        )
        copy.start()
        return copy


class GatherTp:
    def __init__(self, send, buf, rows, part):
        self.send, self.buf, self.rows, self.part = send, buf, rows, part
        self.core = place()[4]
        self.done = []
        self.sib = []

    def slot(self, k):
        return self.buf.at[self.core, pl.ds(k * self.rows, self.rows)]

    def go(self, src, dst, h, off):
        copy = self.send(self.part(self.slot(src), h), self.part(self.slot(dst), h), off)
        self.done.append(copy)
        return copy

    def sibling(self, k):
        self.sib.append(self.send(self.slot(k), self.slot(k), CORE))

    def p1(self):
        self.z = [self.go(0, 4, 0, ZH), self.go(0, 4, 1, ZH)]
        self.p0 = self.go(0, 1, 0, YP)
        self.m1 = self.go(0, 2, 1, YM)
        self.p1_ = self.go(0, 1, 1, YP)
        self.m0 = self.go(0, 2, 0, YM)
        self.sibling(0)

    def p2(self):
        self.z[0].wait_recv()
        self.q0 = self.go(4, 5, 0, YP)
        self.z[1].wait_recv()
        self.n1 = self.go(4, 6, 1, YM)
        self.q1 = self.go(4, 5, 1, YP)
        self.n0 = self.go(4, 6, 0, YM)
        self.sibling(4)

    def p3(self):
        self.p0.wait_recv()
        self.f1 = self.go(1, 3, 0, YP)
        self.m1.wait_recv()
        self.f2 = self.go(2, 3, 1, YM)
        self.p1_.wait_recv()
        self.sibling(1)
        self.m0.wait_recv()
        self.sibling(2)
        self.q0.wait_recv()
        self.f3 = self.go(5, 7, 0, YP)
        self.n1.wait_recv()
        self.f4 = self.go(6, 7, 1, YM)

    def p4(self):
        self.f1.wait_recv()
        self.f2.wait_recv()
        self.sibling(3)
        self.q1.wait_recv()
        self.sibling(5)
        self.n0.wait_recv()
        self.sibling(6)
        self.f3.wait_recv()
        self.f4.wait_recv()
        self.sibling(7)

    def p5(self):
        for copy in self.sib:
            copy.wait_recv()
        for copy in self.sib + self.done:
            copy.wait_send()

    def all(self):
        self.p1()
        self.p2()
        self.p3()
        self.p4()
        self.p5()


class GatherRep:
    def __init__(self, send, ref):
        self.send, self.ref = send, ref
        self.first, self.second, self.third = {}, {}, {}

    def go(self, src, dst, j, off):
        return [self.send(a, b, off) for a, b in zip(self.ref(src, j), self.ref(dst, j, off))]

    def a(self, j):
        self.first[j] = (self.go(0, 4, j, ZL), self.go(0, 1, j, XP), self.go(0, 2, j, XM))

    def b(self, j):
        for copies in self.first[j]:
            for copy in copies:
                copy.wait_recv()
        f = self.go(1, 3, j, XP) if j % 2 == 0 else self.go(2, 3, j, XM)
        if (j // 2) % 2 == 0:
            more = (self.go(4, 5, j, XP), self.go(4, 6, j, XM))
        else:
            more = (self.go(1, 5, j, ZL), self.go(2, 6, j, ZL))
        self.second[j] = (f,) + more

    def c(self, j):
        for copies in self.second[j]:
            for copy in copies:
                copy.wait_recv()
        if (j // 2) % 2 == 0:
            self.third[j] = self.go(5, 7, j, XP) if j % 2 == 1 else self.go(6, 7, j, XM)
        else:
            self.third[j] = self.go(3, 7, j, ZL)

    def end(self, j):
        for copy in self.third[j]:
            copy.wait_recv()
        for copies in self.first[j] + self.second[j] + (self.third[j],):
            for copy in copies:
                copy.wait_send()


def columns_part(ref, h):
    return ref.at[:, pl.ds(h * (HALF // 2), HALF // 2)]


def rows_part(ref, h):
    return ref.at[pl.ds(h * (ROWS // 2), ROWS // 2)]


def body(
    scale_up,
    scale_down,
    mine,
    other,
    up_hbm,
    down_hbm,
    out,
    up,
    down,
    down_own,
    sib_prep,
    local,
    tok0,
    tok1,
    pre,
    hid,
    ht0,
    ht1,
    sib_send,
    sib_recv,
    part,
    r_far,
    r_near,
    r_z,
    err0,
    es0,
    es1,
    res,
    send_sems,
    recv_sems,
    copy_sems,
):
    _, _, _, _, core = place()
    me = lax.axis_index("rep")
    send = Sends(send_sems, recv_sems)

    loads = [
        pltpu.make_async_copy(up_hbm, up, copy_sems.at[0]),
        pltpu.make_async_copy(down_hbm, down, copy_sems.at[1]),
    ]
    for h in range(2):
        cols = pl.ds(pl.multiple_of(h * HALF + me * SLICE, SLICE), SLICE)
        loads.append(pltpu.make_async_copy(down_hbm.at[:, cols], down_own.at[h], copy_sems.at[2 + h]))
    for load in loads:
        load.start()

    peers = (CORE, YP, YM, ZH) + REP[1:]
    barrier = pltpu.get_barrier_semaphore()
    for off in peers:
        pl.semaphore_signal(barrier, inc=1, device_id=target(off), device_id_type=MESH)
    pl.semaphore_wait(barrier, len(peers))

    prep = send(other, sib_prep, CORE)
    prep.wait_recv()
    for i in range(4):
        rows = pl.ds(24 * i, 24)
        a, b = mine[rows, :].astype(F32), sib_prep[rows, :].astype(F32)
        first, second = jnp.where(core == 0, a, b), jnp.where(core == 0, b, a)
        local[i] = jnp.concatenate([first, second], axis=0).astype(BF)
    prep.wait_send()
    tok0[core, pl.ds(0, TOK), :] = local[0]
    tok1[core, pl.ds(0, TOK), :] = local[2]

    def preact(tokens):
        pre[...] = jnp.zeros_like(pre)
        for h in range(2):

            @pl.loop(0, HALF // 512)
            def _(k):
                cols = pl.ds(pl.multiple_of(k * 512, 512), 512)
                rows = pl.ds(pl.multiple_of(h * HALF + k * 512, 512), 512)
                pre[...] += jnp.dot(tokens[h, :, cols], up[rows, :], preferred_element_type=F32)

    def activate(ht):
        @pl.loop(0, 7)
        def _(k):
            cols = pl.ds(pl.multiple_of(k * 128, 128), 128)
            v = pre[:, cols] * scale_up
            hidden = (v * jax.nn.sigmoid(v)).astype(BF)
            hid[:, cols] = hidden
            ht[0, cols, :] = hidden.T

    def layer_out(base, width, store):
        @pl.loop(0, width // 512)
        def _(k):
            inner = pl.multiple_of(k * 512, 512)
            cols = pl.ds(pl.multiple_of(base + inner, 512), 512)
            store(inner, jnp.dot(hid[...], down[:, cols], preferred_element_type=F32))

    def forward_down(between):
        sib = []
        for h in range(2):

            def to_sibling(inner, value, h=h):
                sib_send[h, :, pl.ds(inner, 512)] = value.astype(BF)

            layer_out((1 - core) * HALF + h * 1024, 1024, to_sibling)
            sib.append(send(sib_send.at[h], sib_recv.at[h], CORE))
        between()
        for h in range(2):
            sib[h].wait_recv()

            def to_part(inner, value, h=h):
                total = value + sib_recv[h, :, pl.ds(inner, 512)].astype(F32)
                part[h, :, pl.ds(inner, 512)] = total.astype(BF)

            layer_out(core * HALF + h * 1024, 1024, to_part)
        for copy in sib:
            copy.wait_send()

    def scatter():
        sent = []

        def go(src, dst, off):
            copy = send(src, dst, off)
            sent.append(copy)
            return copy

        def block(k, h):
            return part.at[h, pl.ds(k * TOK, TOK)]

        far, near = {}, {}
        for p in (1, 0):
            far[p, 0] = go(block(4 * p + 3, 0), r_far.at[p, 0], YP)
            far[p, 1] = go(block(4 * p + 3, 1), r_far.at[p, 1], YM)
            near[p, 0, 1] = go(block(4 * p + 2, 1), r_near.at[p, 0, 1], YP)
            near[p, 1, 0] = go(block(4 * p + 1, 0), r_near.at[p, 1, 0], YM)
        for p in (1, 0):
            for d, off in ((0, YP), (1, YM)):
                far[p, d].wait_recv()
                rows = pl.ds((4 * p + 2 - d) * TOK, TOK)
                total = part[d, rows, :].astype(F32) + r_far[p, d].astype(F32)
                part[d, rows, :] = total.astype(BF)
                near[p, d, d] = go(block(4 * p + 2 - d, d), r_near.at[p, d, d], off)
        z = []
        for h in range(2):
            near[1, 0, h].wait_recv()
            near[1, 1, h].wait_recv()
            rows = pl.ds(4 * TOK, TOK)
            total = part[h, rows, :].astype(F32) + r_near[1, 0, h].astype(F32) + r_near[1, 1, h].astype(F32)
            part[h, rows, :] = total.astype(BF)
            z.append(go(block(4, h), r_z.at[h], ZH))
        halves = []
        for h in range(2):
            near[0, 0, h].wait_recv()
            near[0, 1, h].wait_recv()
            total = part[h, pl.ds(0, TOK), :].astype(F32) + r_near[0, 0, h].astype(F32) + r_near[0, 1, h].astype(F32)
            z[h].wait_recv()
            halves.append(total + r_z[h].astype(F32))
        for copy in sent:
            copy.wait_send()
        return halves

    def error(step, halves, dst, es):
        for h in range(2):
            cols = pl.ds(h * 1024, 1024)
            value = local[2 * step, :, cols].astype(F32) + scale_down * halves[h] - local[2 * step + 1, :, cols].astype(F32)
            dst[:, cols] = value.astype(BF)
        sent = []
        for k in range(1, 8):
            cols = pl.ds(pl.multiple_of(rep_index(REP[k]) * SLICE, SLICE), SLICE)
            sent.append(send(dst.at[:, cols], es.at[core, pl.ds(k * TOK, TOK)], REP[k]))
        cols = pl.ds(pl.multiple_of(me * SLICE, SLICE), SLICE)
        es[core, pl.ds(0, TOK), :] = dst[:, cols]
        return sent

    def hidden_gather(ht):
        size = ht.shape[1] // CHUNKS
        return GatherRep(send, lambda slot, j, off=None: [ht.at[slot, pl.ds(j * size, size)]])

    GatherTp(send, tok0, TOK, columns_part).all()
    late = GatherTp(send, tok1, TOK, columns_part)
    late.p1()
    loads[0].wait()
    preact(tok0)
    late.p2()
    activate(ht0)
    rep0 = hidden_gather(ht0)
    for j in range(CHUNKS):
        rep0.a(j)
    loads[1].wait()
    forward_down(late.p3)
    halves = scatter()
    late.p4()
    sliced = error(0, halves, err0.at[core, pl.ds(0, TOK)], es0)
    gather = GatherTp(send, err0, TOK, columns_part)
    gather.p1()
    for j in range(CHUNKS):
        rep0.b(j)
    gather.p2()
    gather.p3()
    gather.p4()
    gather.p5()
    for copy in sliced:
        copy.wait()
    slices = GatherTp(send, es0, ROWS, rows_part)
    slices.p1()

    @pl.loop(0, 3)
    def _(n):
        rows = pl.ds(pl.multiple_of(n * 128, 128), 128)
        total = jnp.zeros((128, 896), F32)
        for h in range(2):
            for k in range(2):
                cols = pl.ds(k * 1024, 1024)
                total += lax.dot_general(
                    err0[h, rows, cols],
                    down[:, pl.ds(h * HALF + k * 1024, 1024)],
                    (((1,), (1,)), ((), ())),
                    preferred_element_type=F32,
                )
        v = pre[rows, :] * scale_up
        sigma = jax.nn.sigmoid(v)
        hid[rows, :] = (scale_down * total * (sigma * (1.0 + v * (1.0 - sigma)))).astype(BF)

    slices.p2()
    for h in range(2):

        @pl.loop(0, HALF // 256)
        def _(k):
            cols = pl.ds(pl.multiple_of(k * 256, 256), 256)
            rows = pl.ds(pl.multiple_of(h * HALF + k * 256, 256), 256)
            g = jnp.dot(tok0[h, :, cols].T, hid[...], preferred_element_type=F32)
            u = g / (jnp.abs(g) + 0.02 / scale_up)
            up[rows, :] = (0.975 * up[rows, :].astype(F32) - 0.25 * u).astype(BF)

    slices.p3()
    for j in range(CHUNKS):
        rep0.c(j)
    late.p5()
    for h in range(2):

        @pl.loop(0, HALF // 256)
        def _(k):
            cols = pl.ds(pl.multiple_of(k * 256, 256), 256)
            wide = pl.ds(pl.multiple_of(h * HALF + k * 256, 256), 256)
            g = jnp.dot(ht0[0], err0[h, :, cols], preferred_element_type=F32)
            u = g / (jnp.abs(g) + 0.02 / scale_down)
            down[:, wide] = (0.975 * down[:, wide].astype(F32) - 0.25 * u).astype(BF)

    slices.p4()
    for j in range(CHUNKS):
        rep0.end(j)

    preact(tok1)
    activate(ht1)
    rep1 = hidden_gather(ht1)
    for j in range(CHUNKS):
        rep1.a(j)
    forward_down(slices.p5)
    halves = scatter()
    sliced = error(1, halves, local.at[0], es1)
    for j in range(CHUNKS):
        rep1.b(j)
    for copy in sliced:
        copy.wait()
    last = GatherTp(send, es1, ROWS, rows_part)
    last.p1()
    last.p2()
    last.p3()
    for j in range(CHUNKS):
        rep1.c(j)
    last.p4()
    last.p5()
    for j in range(CHUNKS):
        rep1.end(j)
    loads[2].wait()
    loads[3].wait()

    size = 896 // CHUNKS

    def reduce(j, h):
        rows = pl.ds(j * size, size)

        def one(k, total):
            tokens = pl.ds(pl.multiple_of(k * TOK, TOK), TOK)
            e0 = es0_view[h, :, tokens, :].reshape(ROWS, SLICE)
            e1 = es1_view[h, :, tokens, :].reshape(ROWS, SLICE)
            g0 = jnp.dot(ht0[k, rows, :], e0, preferred_element_type=F32)
            g1 = jnp.dot(ht1[k, rows, :], e1, preferred_element_type=F32)
            u0 = g0 / (jnp.abs(g0) + 0.02 / scale_down)
            first = (0.09 / 0.19) * g0 + (0.1 / 0.19) * g1
            second = (0.0475 / 0.0975) * (g0 * g0) + (0.05 / 0.0975) * (g1 * g1)
            u1 = first / (jnp.sqrt(second) + 0.02 / scale_down)
            return total + (0.975 * u0 + u1)

        total = lax.fori_loop(0, 8, one, jnp.zeros((size, SLICE), F32))
        w = down_own[h, rows, :].astype(F32)
        average = (1.0 - 0.975 * 0.975) * w + (0.25 / 8.0) * total
        res[h, rows, :] = (w - 0.7 * 1.9 * average).astype(BF)

    es0_view = es0.reshape(2, 8, ROWS, SLICE)
    es1_view = es1.reshape(2, 8, ROWS, SLICE)

    def pieces(slot, j, off=None):
        rows = pl.ds(j * size, size)
        if slot == 0:
            return [res.at[h, rows] for h in range(2)]
        back = REP[slot]
        shift = off if off is not None else (0, 0)
        r = rep_index((shift[0] - back[0] + 4, shift[1] - back[1] + 2))
        return [out.at[rows, pl.ds(pl.multiple_of(h * HALF + r * SLICE, SLICE), SLICE)] for h in range(2)]

    final = GatherRep(send, pieces)
    own = []
    for j in range(CHUNKS):
        for h in range(2):
            reduce(j, h)
        final.a(j)
        for h in range(2):
            cols = pl.ds(pl.multiple_of(h * HALF + me * SLICE, SLICE), SLICE)
            rows = pl.ds(j * size, size)
            own.append(pltpu.make_async_copy(res.at[h, rows], out.at[rows, cols], copy_sems.at[4 + 2 * j + h]))
            own[-1].start()
        if j >= 1:
            final.b(j - 1)
        if j >= 2:
            final.c(j - 2)
    final.b(CHUNKS - 1)
    final.c(CHUNKS - 2)
    final.c(CHUNKS - 1)
    for j in range(CHUNKS):
        final.end(j)
    for copy in own:
        copy.wait()


SEMS = 300


def round_kernel(mine, other, up_weight, down_weight, scale_up, scale_down):
    vmem, anywhere = pl.BlockSpec(memory_space=pltpu.VMEM), pl.BlockSpec(memory_space=pl.ANY)
    width, hidden = up_weight.shape
    return pl.pallas_call(
        functools.partial(body, scale_up, scale_down),
        out_shape=jax.ShapeDtypeStruct(down_weight.shape, BF),
        in_specs=[vmem, vmem, anywhere, anywhere],
        out_specs=anywhere,
        scratch_shapes=[
            pltpu.VMEM((width, hidden), BF),
            pltpu.VMEM((hidden, width), BF),
            pltpu.VMEM((2, hidden, SLICE), BF),
            pltpu.VMEM((96, HALF), BF),
            pltpu.VMEM((4, TOK, HALF), BF),
            pltpu.VMEM((2, ROWS, HALF), BF),
            pltpu.VMEM((2, ROWS, HALF), BF),
            pltpu.VMEM((ROWS, hidden), F32),
            pltpu.VMEM((ROWS, hidden), BF),
            pltpu.VMEM((8, hidden, ROWS), BF),
            pltpu.VMEM((8, hidden, ROWS), BF),
            pltpu.VMEM((2, ROWS, HALF // 2), BF),
            pltpu.VMEM((2, ROWS, HALF // 2), BF),
            pltpu.VMEM((2, ROWS, HALF // 2), BF),
            pltpu.VMEM((2, 2, TOK, HALF // 2), BF),
            pltpu.VMEM((2, 2, 2, TOK, HALF // 2), BF),
            pltpu.VMEM((2, TOK, HALF // 2), BF),
            pltpu.VMEM((2, ROWS, HALF), BF),
            pltpu.VMEM((2, 8 * ROWS, SLICE), BF),
            pltpu.VMEM((2, 8 * ROWS, SLICE), BF),
            pltpu.VMEM((2, hidden, SLICE), BF),
            pltpu.SemaphoreType.DMA((SEMS,)),
            pltpu.SemaphoreType.DMA((SEMS,)),
            pltpu.SemaphoreType.DMA((4 + 2 * CHUNKS,)),
        ],
        compiler_params=pltpu.CompilerParams(
            collective_id=0, has_side_effects=True, vmem_limit_bytes=62 * 2**20
        ),
    )(mine, other, up_weight, down_weight)


def per_device(pool_tokens, pool_targets, pick, up_weight, down_weight):
    core = lax.axis_index("tp") % 2
    chosen = pick[0]
    rows = jnp.concatenate(
        [jnp.take(pool, chosen[step], axis=0) for step in range(2) for pool in (pool_tokens, pool_targets)], axis=0
    )
    mine = lax.dynamic_slice_in_dim(rows, core * HALF, HALF, axis=1)
    other = lax.dynamic_slice_in_dim(rows, (1 - core) * HALF, HALF, axis=1)
    scale_up = 1.0 / math.sqrt(up_weight.shape[0])
    scale_down = 1.0 / math.sqrt(up_weight.shape[1] * lax.axis_size("tp"))
    return round_kernel(mine, other, up_weight, down_weight, scale_up, scale_down)


def solution(mesh):
    in_specs = (P("tp", None), P("tp", None), P("rep", None, "tp"), P(None, "tp"), P("tp", None))
    return jax.shard_map(per_device, mesh=mesh, in_specs=in_specs, out_specs=P("tp", None), check_vma=False)
```

time: 784 us -> 263 us (0.34)
  waiting for transfers between devices: 638 us -> 0 us
  Pallas kernels: 0 us -> 249 us
  matrix products: 102 us -> 0 us
  other arithmetic: 18.2 us -> 1 us
  between operations: 13.8 us -> 0.07 us
  local copies, waits for them, and re-layouts: 2.98 us -> 11 us
    psum x1 -> x0, waiting for transfers between devices: 299 us -> none  [per_device(): lax.psum(delta.astype(jnp.bfloat16), 'rep').astype(jnp.float32) / replicas]
    pallas_call x0 -> x1, Pallas kernels: none -> 249 us  [round_kernel(): pl.pallas_call(functools.partial(body, scale_up, scale_down), out_shape=j...]
    all_gather x4 -> x0, waiting for transfers between devices: 192 us -> none  [the longest x2 102 us: forward(): error_all = lax.all_gather(error, 'tp', axis=0, tiled=True)]
    reduce_scatter x2 -> x0, waiting for transfers between devices: 147 us -> none  [forward(): lax.psum_scatter((scale_down * jnp.dot(hidden, down_cast, preferred_eleme...]
    dot_general x7 -> x0, matrix products: 102 us -> none  [the longest x2 40.5 us: forward(): lax.dot_general(hidden, error_all, (((0,), (0,)), ((), ())), preferred_el...]
    convert_element_type x3 -> x0, other arithmetic: 16 us -> none  [the longest x1 12.4 us: per_device(): return outer_step(down_start, average).astype(jnp.bfloat16)]
  transfers between devices with their start and end apart: 7 -> 0, of which waited for: 7 -> 0; matrix products, arithmetic and copies ran while one was open for 3% -> 0% of each run, Pallas kernels for 0% -> 0%
where the time goes in v1:
time: 263 us; the launch traced here: 261 us
  Pallas kernels  249 us (95%)
  local copies, waits for them, and re-layouts  11 us (4%)
    pallas_call x1, Pallas kernels, round_kernel(): pl.pallas_call(functools.partial(body, scale_up, scale_down), out_shape=j...  249 us
    unnamed x5, local copies, waits for them, and re-layouts  7.34 us

profile of v1, /device:TPU:0, one launch (start us, length us, event | category | flops | bytes accessed | tf_op | source)
XLA Modules:
  0.0 261.3 jit_solution(13555222012418735025)
XLA Ops:
  0.0 0.0 copy-start
  0.0 0.0 copy-start.1
  0.0 0.8 compare_and_fusion.1
  0.8 0.3 copy-done
  1.1 0.7 gather_fusion.3
  1.7 0.0 copy-done.1
  1.8 0.7 gather_fusion.2
  2.4 0.7 gather_fusion.1
  3.1 0.7 gather_fusion
  3.8 0.1 broadcast_select_fusion.1
  3.9 0.1 pad_maximum_fusion
  4.0 1.0 constant_dynamic-slice_fusion
  4.9 249.3 %shard_map.55 = bf16[896,4096]{1,0:T(8,128)(2,1)} custom-call(bf16[96,2048]{1,0:T(8,128)(2,1)} %get-tuple-element.11.mine, bf16[96,2048]{1,0:T(8,128)(2,1)} %get-tuple-element.10.other, bf16[4096,896]{1,0:T(8,128)(2,1)} %up_hbm.1, bf16[896,4096]{1,0:T(8,128)(2,1)} %down_hbm.1), custom_call_target="tpu_custom_call" | custom-call | tf_op jit(solution)/shard_map/pallas_call | solution.py:518
  254.2 7.1 %copy.7 = bf16[896,4096]{1,0:T(8,128)(2,1)} copy(bf16[896,4096]{1,0:T(8,128)(2,1)} %shard_map.55) | data formatting | bytes 14680064
  (2 shorter events, 0.0 us)
Async XLA Ops:
  0.0 1.1 copy-start
  0.0 1.7 copy-start.1

commit v2 on v1

--- a/solution.py
+++ b/solution.py
@@ -38,6 +38,15 @@
     _, _, zh, y, core = place()
     tp = (((zh + off[2]) % 2) * 4 + (y + off[3] + 4) % 4) * 2 + (core + off[4]) % 2
     return (rep_index(off), tp)
+
+
+def inverse(v):
+    return pl.reciprocal(v, approx=True)
+
+
+def run(hook):
+    if hook is not None:
+        hook()
 
 
 class Sends:
@@ -135,8 +144,8 @@
 
 
 class GatherRep:
-    def __init__(self, send, ref):
-        self.send, self.ref = send, ref
+    def __init__(self, send, ref, late_z):
+        self.send, self.ref, self.late_z = send, ref, late_z
         self.first, self.second, self.third = {}, {}, {}
 
     def go(self, src, dst, j, off):
@@ -150,7 +159,7 @@
             for copy in copies:
                 copy.wait_recv()
         f = self.go(1, 3, j, XP) if j % 2 == 0 else self.go(2, 3, j, XM)
-        if (j // 2) % 2 == 0:
+        if j not in self.late_z:
             more = (self.go(4, 5, j, XP), self.go(4, 6, j, XM))
         else:
             more = (self.go(1, 5, j, ZL), self.go(2, 6, j, ZL))
@@ -160,7 +169,7 @@
         for copies in self.second[j]:
             for copy in copies:
                 copy.wait_recv()
-        if (j // 2) % 2 == 0:
+        if j not in self.late_z:
             self.third[j] = self.go(5, 7, j, XP) if j % 2 == 1 else self.go(6, 7, j, XM)
         else:
             self.third[j] = self.go(3, 7, j, ZL)
@@ -184,14 +193,16 @@
 def body(
     scale_up,
     scale_down,
-    mine,
-    other,
+    pick,
+    pool_tokens,
+    pool_targets,
     up_hbm,
     down_hbm,
     out,
     up,
     down,
     down_own,
+    sib_out,
     sib_prep,
     local,
     tok0,
@@ -209,7 +220,9 @@
     err0,
     es0,
     es1,
-    res,
+    acc,
+    grad0,
+    base,
     send_sems,
     recv_sems,
     copy_sems,
@@ -232,15 +245,38 @@
     barrier = pltpu.get_barrier_semaphore()
     for off in peers:
         pl.semaphore_signal(barrier, inc=1, device_id=target(off), device_id_type=MESH)
+
+    def picked(step, pool, cols):
+        row = lax.broadcasted_iota(jnp.int32, (24, 64), 0)
+        col = lax.broadcasted_iota(jnp.int32, (24, 64), 1)
+        chosen = jnp.zeros((24, 64), jnp.int32)
+        for i in range(24):
+            chosen = jnp.where(row == i, pick[step, i], chosen)
+        return jnp.dot((chosen == col).astype(F32).astype(BF), pool[:, cols], preferred_element_type=F32)
+
+    sources = [(step, pool) for step in range(2) for pool in (pool_tokens, pool_targets)]
+
+    @pl.loop(0, HALF // 512)
+    def _(k):
+        inner = pl.ds(pl.multiple_of(k * 512, 512), 512)
+        cols = pl.ds(pl.multiple_of((1 - core) * HALF + k * 512, 512), 512)
+        sib_out[:, inner] = jnp.concatenate([picked(*source, cols) for source in sources], axis=0).astype(BF)
+
     pl.semaphore_wait(barrier, len(peers))
 
-    prep = send(other, sib_prep, CORE)
+    prep = send(sib_out, sib_prep, CORE)
     prep.wait_recv()
-    for i in range(4):
-        rows = pl.ds(24 * i, 24)
-        a, b = mine[rows, :].astype(F32), sib_prep[rows, :].astype(F32)
-        first, second = jnp.where(core == 0, a, b), jnp.where(core == 0, b, a)
-        local[i] = jnp.concatenate([first, second], axis=0).astype(BF)
+
+    @pl.loop(0, HALF // 512)
+    def _(k):
+        inner = pl.ds(pl.multiple_of(k * 512, 512), 512)
+        cols = pl.ds(pl.multiple_of(core * HALF + k * 512, 512), 512)
+        theirs = sib_prep[:, inner].astype(F32)
+        for i, source in enumerate(sources):
+            a, b = picked(*source, cols), theirs[24 * i : 24 * i + 24]
+            first, second = jnp.where(core == 0, a, b), jnp.where(core == 0, b, a)
+            local[i, :, inner] = jnp.concatenate([first, second], axis=0).astype(BF)
+
     prep.wait_send()
     tok0[core, pl.ds(0, TOK), :] = local[0]
     tok1[core, pl.ds(0, TOK), :] = local[2]
@@ -292,7 +328,7 @@
         for copy in sib:
             copy.wait_send()
 
-    def scatter():
+    def scatter(hooks=(None, None, None)):
         sent = []
 
         def go(src, dst, off):
@@ -309,6 +345,7 @@
             far[p, 1] = go(block(4 * p + 3, 1), r_far.at[p, 1], YM)
             near[p, 0, 1] = go(block(4 * p + 2, 1), r_near.at[p, 0, 1], YP)
             near[p, 1, 0] = go(block(4 * p + 1, 0), r_near.at[p, 1, 0], YM)
+        run(hooks[0])
         for p in (1, 0):
             for d, off in ((0, YP), (1, YM)):
                 far[p, d].wait_recv()
@@ -316,6 +353,7 @@
                 total = part[d, rows, :].astype(F32) + r_far[p, d].astype(F32)
                 part[d, rows, :] = total.astype(BF)
                 near[p, d, d] = go(block(4 * p + 2 - d, d), r_near.at[p, d, d], off)
+        run(hooks[1])
         z = []
         for h in range(2):
             near[1, 0, h].wait_recv()
@@ -324,6 +362,7 @@
             total = part[h, rows, :].astype(F32) + r_near[1, 0, h].astype(F32) + r_near[1, 1, h].astype(F32)
             part[h, rows, :] = total.astype(BF)
             z.append(go(block(4, h), r_z.at[h], ZH))
+        run(hooks[2])
         halves = []
         for h in range(2):
             near[0, 0, h].wait_recv()
@@ -350,7 +389,7 @@
 
     def hidden_gather(ht):
         size = ht.shape[1] // CHUNKS
-        return GatherRep(send, lambda slot, j, off=None: [ht.at[slot, pl.ds(j * size, size)]])
+        return GatherRep(send, lambda slot, j, off=None: [ht.at[slot, pl.ds(j * size, size)]], (3,))
 
     GatherTp(send, tok0, TOK, columns_part).all()
     late = GatherTp(send, tok1, TOK, columns_part)
@@ -367,51 +406,76 @@
     halves = scatter()
     late.p4()
     sliced = error(0, halves, err0.at[core, pl.ds(0, TOK)], es0)
+    def transpose_tokens(quarter):
+        h = quarter // 2
+
+        @pl.loop(0, 4)
+        def _(k):
+            inner = pl.multiple_of(quarter % 2 * 1024 + k * 256, 256)
+            wide = pl.multiple_of(h * HALF + inner, 256)
+            turned = tok0[h, :, pl.ds(inner, 256)].T
+            grad0[pl.ds(wide, 256), :] = turned[:, :256]
+            grad0[pl.ds(2 * HALF + wide, 256), pl.ds(0, 128)] = turned[:, 256:]
+
     gather = GatherTp(send, err0, TOK, columns_part)
     gather.p1()
+    transpose_tokens(0)
     for j in range(CHUNKS):
         rep0.b(j)
     gather.p2()
+    transpose_tokens(1)
     gather.p3()
+    transpose_tokens(2)
     gather.p4()
+    transpose_tokens(3)
     gather.p5()
     for copy in sliced:
         copy.wait()
     slices = GatherTp(send, es0, ROWS, rows_part)
     slices.p1()
 
+    acc[...] = jnp.zeros_like(acc)
+    for h in range(2):
+
+        @pl.loop(0, HALF // 512)
+        def _(k):
+            cols = pl.ds(pl.multiple_of(k * 512, 512), 512)
+            wide = pl.ds(pl.multiple_of(h * HALF + k * 512, 512), 512)
+            acc[...] += lax.dot_general(
+                err0[h, :, cols], down[:, wide], (((1,), (1,)), ((), ())), preferred_element_type=F32
+            )
+
     @pl.loop(0, 3)
     def _(n):
         rows = pl.ds(pl.multiple_of(n * 128, 128), 128)
-        total = jnp.zeros((128, 896), F32)
-        for h in range(2):
-            for k in range(2):
-                cols = pl.ds(k * 1024, 1024)
-                total += lax.dot_general(
-                    err0[h, rows, cols],
-                    down[:, pl.ds(h * HALF + k * 1024, 1024)],
-                    (((1,), (1,)), ((), ())),
-                    preferred_element_type=F32,
-                )
         v = pre[rows, :] * scale_up
         sigma = jax.nn.sigmoid(v)
-        hid[rows, :] = (scale_down * total * (sigma * (1.0 + v * (1.0 - sigma)))).astype(BF)
+        hid[rows, :] = (scale_down * acc[rows, :] * (sigma * (1.0 + v * (1.0 - sigma)))).astype(BF)
 
     slices.p2()
     for h in range(2):
 
         @pl.loop(0, HALF // 256)
         def _(k):
-            cols = pl.ds(pl.multiple_of(k * 256, 256), 256)
-            rows = pl.ds(pl.multiple_of(h * HALF + k * 256, 256), 256)
-            g = jnp.dot(tok0[h, :, cols].T, hid[...], preferred_element_type=F32)
-            u = g / (jnp.abs(g) + 0.02 / scale_up)
+            wide = pl.multiple_of(h * HALF + k * 256, 256)
+            rows = pl.ds(wide, 256)
+            g = jnp.dot(grad0[rows, :], hid[pl.ds(0, 256), :], preferred_element_type=F32)
+            g += jnp.dot(
+                grad0[pl.ds(2 * HALF + wide, 256), pl.ds(0, 128)], hid[pl.ds(256, 128), :], preferred_element_type=F32
+            )
+            u = g * inverse(jnp.abs(g) + 0.02 / scale_up)
             up[rows, :] = (0.975 * up[rows, :].astype(F32) - 0.25 * u).astype(BF)
 
     slices.p3()
     for j in range(CHUNKS):
         rep0.c(j)
     late.p5()
+
+    preact(tok1)
+    activate(ht1)
+    rep1 = hidden_gather(ht1)
+    for j in range(CHUNKS):
+        rep1.a(j)
     for h in range(2):
 
         @pl.loop(0, HALF // 256)
@@ -419,111 +483,134 @@
             cols = pl.ds(pl.multiple_of(k * 256, 256), 256)
             wide = pl.ds(pl.multiple_of(h * HALF + k * 256, 256), 256)
             g = jnp.dot(ht0[0], err0[h, :, cols], preferred_element_type=F32)
-            u = g / (jnp.abs(g) + 0.02 / scale_down)
+            u = g * inverse(jnp.abs(g) + 0.02 / scale_down)
             down[:, wide] = (0.975 * down[:, wide].astype(F32) - 0.25 * u).astype(BF)
 
     slices.p4()
     for j in range(CHUNKS):
         rep0.end(j)
 
-    preact(tok1)
-    activate(ht1)
-    rep1 = hidden_gather(ht1)
-    for j in range(CHUNKS):
-        rep1.a(j)
+    es0_view = es0.reshape(2, 8, ROWS, SLICE)
+    es1_view = es1.reshape(2, 8, ROWS, SLICE)
+    size = 896 // CHUNKS
+
+    def slice_of(view, h, k):
+        tokens = pl.ds(k * TOK if isinstance(k, int) else pl.multiple_of(k * TOK, TOK), TOK)
+        return view[h, :, tokens, :].reshape(ROWS, SLICE)
+
+    def first_update(k):
+        for h in range(2):
+            e = slice_of(es0_view, h, k)
+
+            @pl.loop(0, CHUNKS)
+            def _(j):
+                rows = pl.ds(pl.multiple_of(j * size, size), size)
+                kept = pl.ds(pl.multiple_of((k * 2 + h) * 896 + j * size, 32), size)
+                g = jnp.dot(ht0[k, rows, :], e, preferred_element_type=F32)
+                u = g * inverse(jnp.abs(g) + 0.02 / scale_down)
+                grad0[kept, :] = g.astype(BF)
+                if k == 0:
+                    base[h, rows, :] = 0.975 * u
+                else:
+                    base[h, rows, :] += 0.975 * u
+
+    def both(k, then=None):
+        def hook():
+            first_update(k)
+            run(then)
+
+        return hook
+
     forward_down(slices.p5)
-    halves = scatter()
+    rep1.b(0)
+    halves = scatter((both(0, lambda: rep1.b(1)), both(1, lambda: rep1.b(2)), both(2, lambda: rep1.b(3))))
     sliced = error(1, halves, local.at[0], es1)
-    for j in range(CHUNKS):
-        rep1.b(j)
+    rep1.c(0)
+    first_update(3)
     for copy in sliced:
         copy.wait()
     last = GatherTp(send, es1, ROWS, rows_part)
     last.p1()
+    rep1.c(1)
+    first_update(4)
     last.p2()
+    rep1.c(2)
+    first_update(5)
     last.p3()
-    for j in range(CHUNKS):
-        rep1.c(j)
+    rep1.c(3)
+    first_update(6)
     last.p4()
+    first_update(7)
     last.p5()
     for j in range(CHUNKS):
         rep1.end(j)
     loads[2].wait()
     loads[3].wait()
 
-    size = 896 // CHUNKS
-
     def reduce(j, h):
         rows = pl.ds(j * size, size)
 
         def one(k, total):
-            tokens = pl.ds(pl.multiple_of(k * TOK, TOK), TOK)
-            e0 = es0_view[h, :, tokens, :].reshape(ROWS, SLICE)
-            e1 = es1_view[h, :, tokens, :].reshape(ROWS, SLICE)
-            g0 = jnp.dot(ht0[k, rows, :], e0, preferred_element_type=F32)
-            g1 = jnp.dot(ht1[k, rows, :], e1, preferred_element_type=F32)
-            u0 = g0 / (jnp.abs(g0) + 0.02 / scale_down)
+            g0 = grad0[pl.ds(pl.multiple_of((k * 2 + h) * 896 + j * size, 32), size), :].astype(F32)
+            g1 = jnp.dot(ht1[k, rows, :], slice_of(es1_view, h, k), preferred_element_type=F32)
             first = (0.09 / 0.19) * g0 + (0.1 / 0.19) * g1
             second = (0.0475 / 0.0975) * (g0 * g0) + (0.05 / 0.0975) * (g1 * g1)
-            u1 = first / (jnp.sqrt(second) + 0.02 / scale_down)
-            return total + (0.975 * u0 + u1)
-
-        total = lax.fori_loop(0, 8, one, jnp.zeros((size, SLICE), F32))
+            root = second * lax.rsqrt(jnp.maximum(second, 1e-30))
+            return total + first * inverse(root + 0.02 / scale_down)
+
+        total = lax.fori_loop(0, 8, one, base[h, rows, :])
         w = down_own[h, rows, :].astype(F32)
         average = (1.0 - 0.975 * 0.975) * w + (0.25 / 8.0) * total
-        res[h, rows, :] = (w - 0.7 * 1.9 * average).astype(BF)
-
-    es0_view = es0.reshape(2, 8, ROWS, SLICE)
-    es1_view = es1.reshape(2, 8, ROWS, SLICE)
-
-    def pieces(slot, j, off=None):
-        rows = pl.ds(j * size, size)
+        down_own[h, rows, :] = (w - 0.7 * 1.9 * average).astype(BF)
+
+    def pieces(slot, n, off=None):
+        h, rows = n // CHUNKS, pl.ds(n % CHUNKS * size, size)
         if slot == 0:
-            return [res.at[h, rows] for h in range(2)]
+            return [down_own.at[h, rows]]
         back = REP[slot]
         shift = off if off is not None else (0, 0)
         r = rep_index((shift[0] - back[0] + 4, shift[1] - back[1] + 2))
-        return [out.at[rows, pl.ds(pl.multiple_of(h * HALF + r * SLICE, SLICE), SLICE)] for h in range(2)]
-
-    final = GatherRep(send, pieces)
+        return [out.at[rows, pl.ds(pl.multiple_of(h * HALF + r * SLICE, SLICE), SLICE)]]
+
+    final = GatherRep(send, pieces, (0, 3, 6))
     own = []
-    for j in range(CHUNKS):
-        for h in range(2):
+    total = 2 * CHUNKS
+    for n in range(total + LAG_C):
+        if n < total:
+            h, j = n // CHUNKS, n % CHUNKS
             reduce(j, h)
-        final.a(j)
-        for h in range(2):
+            final.a(n)
             cols = pl.ds(pl.multiple_of(h * HALF + me * SLICE, SLICE), SLICE)
             rows = pl.ds(j * size, size)
-            own.append(pltpu.make_async_copy(res.at[h, rows], out.at[rows, cols], copy_sems.at[4 + 2 * j + h]))
+            own.append(pltpu.make_async_copy(down_own.at[h, rows], out.at[rows, cols], copy_sems.at[4 + n]))
             own[-1].start()
-        if j >= 1:
-            final.b(j - 1)
-        if j >= 2:
-            final.c(j - 2)
-    final.b(CHUNKS - 1)
-    final.c(CHUNKS - 2)
-    final.c(CHUNKS - 1)
-    for j in range(CHUNKS):
-        final.end(j)
+        if 0 <= n - LAG_B < total:
+            final.b(n - LAG_B)
+        if 0 <= n - LAG_C < total:
+            final.c(n - LAG_C)
+    for n in range(total):
+        final.end(n)
     for copy in own:
         copy.wait()
 
 
+LAG_B, LAG_C = 1, 2
 SEMS = 300
 
 
-def round_kernel(mine, other, up_weight, down_weight, scale_up, scale_down):
+def round_kernel(pick, pool_tokens, pool_targets, up_weight, down_weight, scale_up, scale_down):
     vmem, anywhere = pl.BlockSpec(memory_space=pltpu.VMEM), pl.BlockSpec(memory_space=pl.ANY)
     width, hidden = up_weight.shape
     return pl.pallas_call(
         functools.partial(body, scale_up, scale_down),
         out_shape=jax.ShapeDtypeStruct(down_weight.shape, BF),
-        in_specs=[vmem, vmem, anywhere, anywhere],
+        in_specs=[pl.BlockSpec(memory_space=pltpu.SMEM), vmem, vmem, anywhere, anywhere],
         out_specs=anywhere,
         scratch_shapes=[
             pltpu.VMEM((width, hidden), BF),
             pltpu.VMEM((hidden, width), BF),
             pltpu.VMEM((2, hidden, SLICE), BF),
+            pltpu.VMEM((96, HALF), BF),
             pltpu.VMEM((96, HALF), BF),
             pltpu.VMEM((4, TOK, HALF), BF),
             pltpu.VMEM((2, ROWS, HALF), BF),
@@ -541,7 +628,9 @@
             pltpu.VMEM((2, ROWS, HALF), BF),
             pltpu.VMEM((2, 8 * ROWS, SLICE), BF),
             pltpu.VMEM((2, 8 * ROWS, SLICE), BF),
-            pltpu.VMEM((2, hidden, SLICE), BF),
+            pltpu.VMEM((ROWS, hidden), F32),
+            pltpu.VMEM((16 * hidden, SLICE), BF),
+            pltpu.VMEM((2, hidden, SLICE), F32),
             pltpu.SemaphoreType.DMA((SEMS,)),
             pltpu.SemaphoreType.DMA((SEMS,)),
             pltpu.SemaphoreType.DMA((4 + 2 * CHUNKS,)),
@@ -549,20 +638,13 @@
         compiler_params=pltpu.CompilerParams(
             collective_id=0, has_side_effects=True, vmem_limit_bytes=62 * 2**20
         ),
-    )(mine, other, up_weight, down_weight)
+    )(pick, pool_tokens, pool_targets, up_weight, down_weight)
 
 
 def per_device(pool_tokens, pool_targets, pick, up_weight, down_weight):
-    core = lax.axis_index("tp") % 2
-    chosen = pick[0]
-    rows = jnp.concatenate(
-        [jnp.take(pool, chosen[step], axis=0) for step in range(2) for pool in (pool_tokens, pool_targets)], axis=0
-    )
-    mine = lax.dynamic_slice_in_dim(rows, core * HALF, HALF, axis=1)
-    other = lax.dynamic_slice_in_dim(rows, (1 - core) * HALF, HALF, axis=1)
     scale_up = 1.0 / math.sqrt(up_weight.shape[0])
     scale_down = 1.0 / math.sqrt(up_weight.shape[1] * lax.axis_size("tp"))
-    return round_kernel(mine, other, up_weight, down_weight, scale_up, scale_down)
+    return round_kernel(pick[0], pool_tokens, pool_targets, up_weight, down_weight, scale_up, scale_down)
 
 
 def solution(mesh):

time: 263 us -> 232 us (0.88)
  Pallas kernels: 249 us -> 224 us
  local copies, waits for them, and re-layouts: 11 us -> 7.08 us
    pallas_call x1, Pallas kernels: 249 us -> 224 us  [round_kernel(): pl.pallas_call(functools.partial(body, scale_up, scale_down), out_shape=j...]
    gather x4 -> x0, local copies, waits for them, and re-layouts: 2.66 us -> none  [per_device(): jnp.take(pool, chosen[step], axis=0)]
    unnamed x5 -> x1, local copies, waits for them, and re-layouts: 7.34 us -> 7.08 us
where the time goes in v2:
time: 232 us; the launch traced here: 231 us
  Pallas kernels  224 us (97%)
  local copies, waits for them, and re-layouts  7.08 us (3%)
    pallas_call x1, Pallas kernels, round_kernel(): pl.pallas_call(functools.partial(body, scale_up, scale_down), out_shape=j...  224 us
    unnamed x1, local copies, waits for them, and re-layouts  7.08 us

profile of v2, /device:TPU:0, one launch (start us, length us, event | category | flops | bytes accessed | tf_op | source)
XLA Modules:
  0.0 230.8 jit_solution(14800804741725256081)
XLA Ops:
  0.0 223.7 %shard_map.55 = bf16[896,4096]{1,0:T(8,128)(2,1)} custom-call(s32[2,24]{1,0:T(2,128)} %bitcast.1, bf16[64,4096]{1,0:T(8,128)(2,1)} %pool_tokens.1, bf16[64,4096]{1,0:T(8,128)(2,1)} %pool_targets.1, bf16[4096,896]{1,0:T(8,128)(2,1)} %up_hbm.1, bf16[896,4096]{1,0:T(8,128)(2,1)} %down_hbm.1), custom_call_target="tpu_custom_call" | custom-call | tf_op jit(solution)/shard_map/pallas_call | solution.py:604
  223.7 7.1 %copy.7 = bf16[896,4096]{1,0:T(8,128)(2,1)} copy(bf16[896,4096]{1,0:T(8,128)(2,1)} %shard_map.55) | data formatting | bytes 14680064

commit v3 on v2

--- a/solution.py
+++ b/solution.py
@@ -202,8 +202,6 @@
     up,
     down,
     down_own,
-    sib_out,
-    sib_prep,
     local,
     tok0,
     tok1,
@@ -258,20 +256,20 @@
 
     @pl.loop(0, HALF // 512)
     def _(k):
-        inner = pl.ds(pl.multiple_of(k * 512, 512), 512)
+        inner = pl.ds(pl.multiple_of(k % 2 * 512, 512), 512)
         cols = pl.ds(pl.multiple_of((1 - core) * HALF + k * 512, 512), 512)
-        sib_out[:, inner] = jnp.concatenate([picked(*source, cols) for source in sources], axis=0).astype(BF)
+        part[k // 2, pl.ds(0, 96), inner] = jnp.concatenate([picked(*source, cols) for source in sources], axis=0).astype(BF)
 
     pl.semaphore_wait(barrier, len(peers))
 
-    prep = send(sib_out, sib_prep, CORE)
+    prep = send(part.at[:, pl.ds(0, 96)], sib_recv.at[:, pl.ds(0, 96)], CORE)
     prep.wait_recv()
 
     @pl.loop(0, HALF // 512)
     def _(k):
         inner = pl.ds(pl.multiple_of(k * 512, 512), 512)
         cols = pl.ds(pl.multiple_of(core * HALF + k * 512, 512), 512)
-        theirs = sib_prep[:, inner].astype(F32)
+        theirs = sib_recv[k // 2, pl.ds(0, 96), pl.ds(pl.multiple_of(k % 2 * 512, 512), 512)].astype(F32)
         for i, source in enumerate(sources):
             a, b = picked(*source, cols), theirs[24 * i : 24 * i + 24]
             first, second = jnp.where(core == 0, a, b), jnp.where(core == 0, b, a)
@@ -285,10 +283,10 @@
         pre[...] = jnp.zeros_like(pre)
         for h in range(2):
 
-            @pl.loop(0, HALF // 512)
+            @pl.loop(0, HALF // 1024, unroll=2)
             def _(k):
-                cols = pl.ds(pl.multiple_of(k * 512, 512), 512)
-                rows = pl.ds(pl.multiple_of(h * HALF + k * 512, 512), 512)
+                cols = pl.ds(pl.multiple_of(k * 1024, 1024), 1024)
+                rows = pl.ds(pl.multiple_of(h * HALF + k * 1024, 1024), 1024)
                 pre[...] += jnp.dot(tokens[h, :, cols], up[rows, :], preferred_element_type=F32)
 
     def activate(ht):
@@ -301,7 +299,7 @@
             ht[0, cols, :] = hidden.T
 
     def layer_out(base, width, store):
-        @pl.loop(0, width // 512)
+        @pl.loop(0, width // 512, unroll=2)
         def _(k):
             inner = pl.multiple_of(k * 512, 512)
             cols = pl.ds(pl.multiple_of(base + inner, 512), 512)
@@ -437,10 +435,10 @@
     acc[...] = jnp.zeros_like(acc)
     for h in range(2):
 
-        @pl.loop(0, HALF // 512)
+        @pl.loop(0, HALF // 1024, unroll=2)
         def _(k):
-            cols = pl.ds(pl.multiple_of(k * 512, 512), 512)
-            wide = pl.ds(pl.multiple_of(h * HALF + k * 512, 512), 512)
+            cols = pl.ds(pl.multiple_of(k * 1024, 1024), 1024)
+            wide = pl.ds(pl.multiple_of(h * HALF + k * 1024, 1024), 1024)
             acc[...] += lax.dot_general(
                 err0[h, :, cols], down[:, wide], (((1,), (1,)), ((), ())), preferred_element_type=F32
             )
@@ -455,7 +453,7 @@
     slices.p2()
     for h in range(2):
 
-        @pl.loop(0, HALF // 256)
+        @pl.loop(0, HALF // 256, unroll=2)
         def _(k):
             wide = pl.multiple_of(h * HALF + k * 256, 256)
             rows = pl.ds(wide, 256)
@@ -478,7 +476,7 @@
         rep1.a(j)
     for h in range(2):
 
-        @pl.loop(0, HALF // 256)
+        @pl.loop(0, HALF // 256, unroll=2)
         def _(k):
             cols = pl.ds(pl.multiple_of(k * 256, 256), 256)
             wide = pl.ds(pl.multiple_of(h * HALF + k * 256, 256), 256)
@@ -558,7 +556,7 @@
             root = second * lax.rsqrt(jnp.maximum(second, 1e-30))
             return total + first * inverse(root + 0.02 / scale_down)
 
-        total = lax.fori_loop(0, 8, one, base[h, rows, :])
+        total = lax.fori_loop(0, 8, one, base[h, rows, :], unroll=2)
         w = down_own[h, rows, :].astype(F32)
         average = (1.0 - 0.975 * 0.975) * w + (0.25 / 8.0) * total
         down_own[h, rows, :] = (w - 0.7 * 1.9 * average).astype(BF)
@@ -594,7 +592,7 @@
         copy.wait()
 
 
-LAG_B, LAG_C = 1, 2
+LAG_B, LAG_C = 2, 3
 SEMS = 300
 
 
@@ -610,8 +608,6 @@
             pltpu.VMEM((width, hidden), BF),
             pltpu.VMEM((hidden, width), BF),
             pltpu.VMEM((2, hidden, SLICE), BF),
-            pltpu.VMEM((96, HALF), BF),
-            pltpu.VMEM((96, HALF), BF),
             pltpu.VMEM((4, TOK, HALF), BF),
             pltpu.VMEM((2, ROWS, HALF), BF),
             pltpu.VMEM((2, ROWS, HALF), BF),
@@ -636,7 +632,7 @@
             pltpu.SemaphoreType.DMA((4 + 2 * CHUNKS,)),
         ],
         compiler_params=pltpu.CompilerParams(
-            collective_id=0, has_side_effects=True, vmem_limit_bytes=62 * 2**20
+            collective_id=0, has_side_effects=True, vmem_limit_bytes=63 * 2**20
         ),
     )(pick, pool_tokens, pool_targets, up_weight, down_weight)
 

time: 232 us -> 228 us (0.983)
  Pallas kernels: 224 us -> 221 us
    pallas_call x1, Pallas kernels: 224 us -> 221 us  [round_kernel(): pl.pallas_call(functools.partial(body, scale_up, scale_down), out_shape=j...]
where the time goes in v3:
time: 228 us
  Pallas kernels  221 us (97%)
  local copies, waits for them, and re-layouts  7.08 us (3%)
    pallas_call x1, Pallas kernels, round_kernel(): pl.pallas_call(functools.partial(body, scale_up, scale_down), out_shape=j...  221 us
    unnamed x1, local copies, waits for them, and re-layouts  7.08 us

profile of v3, /device:TPU:0, one launch (start us, length us, event | category | flops | bytes accessed | tf_op | source)
XLA Modules:
  0.0 227.9 jit_solution(2771080586142457158)
XLA Ops:
  0.0 220.9 %shard_map.55 = bf16[896,4096]{1,0:T(8,128)(2,1)} custom-call(s32[2,24]{1,0:T(2,128)} %bitcast.1, bf16[64,4096]{1,0:T(8,128)(2,1)} %pool_tokens.1, bf16[64,4096]{1,0:T(8,128)(2,1)} %pool_targets.1, bf16[4096,896]{1,0:T(8,128)(2,1)} %up_hbm.1, bf16[896,4096]{1,0:T(8,128)(2,1)} %down_hbm.1), custom_call_target="tpu_custom_call" | custom-call | tf_op jit(solution)/shard_map/pallas_call | solution.py:602
  220.9 7.1 %copy.7 = bf16[896,4096]{1,0:T(8,128)(2,1)} copy(bf16[896,4096]{1,0:T(8,128)(2,1)} %shard_map.55) | data formatting | bytes 14680064

commit v4 on v3

--- a/solution.py
+++ b/solution.py
@@ -265,19 +265,20 @@
     prep = send(part.at[:, pl.ds(0, 96)], sib_recv.at[:, pl.ds(0, 96)], CORE)
     prep.wait_recv()
 
-    @pl.loop(0, HALF // 512)
-    def _(k):
-        inner = pl.ds(pl.multiple_of(k * 512, 512), 512)
-        cols = pl.ds(pl.multiple_of(core * HALF + k * 512, 512), 512)
-        theirs = sib_recv[k // 2, pl.ds(0, 96), pl.ds(pl.multiple_of(k % 2 * 512, 512), 512)].astype(F32)
-        for i, source in enumerate(sources):
-            a, b = picked(*source, cols), theirs[24 * i : 24 * i + 24]
-            first, second = jnp.where(core == 0, a, b), jnp.where(core == 0, b, a)
-            local[i, :, inner] = jnp.concatenate([first, second], axis=0).astype(BF)
-
+    def assemble(which):
+        @pl.loop(0, HALF // 512)
+        def _(k):
+            inner = pl.ds(pl.multiple_of(k * 512, 512), 512)
+            cols = pl.ds(pl.multiple_of(core * HALF + k * 512, 512), 512)
+            theirs = sib_recv[k // 2, pl.ds(0, 96), pl.ds(pl.multiple_of(k % 2 * 512, 512), 512)].astype(F32)
+            for i in which:
+                a, b = picked(*sources[i], cols), theirs[24 * i : 24 * i + 24]
+                first, second = jnp.where(core == 0, a, b), jnp.where(core == 0, b, a)
+                local[i, :, inner] = jnp.concatenate([first, second], axis=0).astype(BF)
+
+    assemble((0,))
     prep.wait_send()
     tok0[core, pl.ds(0, TOK), :] = local[0]
-    tok1[core, pl.ds(0, TOK), :] = local[2]
 
     def preact(tokens):
         pre[...] = jnp.zeros_like(pre)
@@ -389,7 +390,14 @@
         size = ht.shape[1] // CHUNKS
         return GatherRep(send, lambda slot, j, off=None: [ht.at[slot, pl.ds(j * size, size)]], (3,))
 
-    GatherTp(send, tok0, TOK, columns_part).all()
+    gather = GatherTp(send, tok0, TOK, columns_part)
+    gather.p1()
+    assemble((1, 2, 3))
+    tok1[core, pl.ds(0, TOK), :] = local[2]
+    gather.p2()
+    gather.p3()
+    gather.p4()
+    gather.p5()
     late = GatherTp(send, tok1, TOK, columns_part)
     late.p1()
     loads[0].wait()

time: 228 us -> 228 us (level)
  no operation moved by 1% of the time
where the time goes in v4:
time: 228 us
  Pallas kernels  221 us (97%)
  local copies, waits for them, and re-layouts  7.08 us (3%)
    pallas_call x1, Pallas kernels, round_kernel(): pl.pallas_call(functools.partial(body, scale_up, scale_down), out_shape=j...  221 us
    unnamed x1, local copies, waits for them, and re-layouts  7.08 us

profile of v4, /device:TPU:0, one launch (start us, length us, event | category | flops | bytes accessed | tf_op | source)
XLA Modules:
  0.0 227.9 jit_solution(5425000423129448535)
XLA Ops:
  0.0 220.8 %shard_map.55 = bf16[896,4096]{1,0:T(8,128)(2,1)} custom-call(s32[2,24]{1,0:T(2,128)} %bitcast.1, bf16[64,4096]{1,0:T(8,128)(2,1)} %pool_tokens.1, bf16[64,4096]{1,0:T(8,128)(2,1)} %pool_targets.1, bf16[4096,896]{1,0:T(8,128)(2,1)} %up_hbm.1, bf16[896,4096]{1,0:T(8,128)(2,1)} %down_hbm.1), custom_call_target="tpu_custom_call" | custom-call | tf_op jit(solution)/shard_map/pallas_call | solution.py:610
  220.8 7.1 %copy.7 = bf16[896,4096]{1,0:T(8,128)(2,1)} copy(bf16[896,4096]{1,0:T(8,128)(2,1)} %shard_map.55) | data formatting | bytes 14680064
